TPU v7x, 256 devices: a whole 4x4x8 slice. The times are simulated.
256 devices in a mesh: row: 32 (over x, y, core), col: 8 (over z).
Axes of the slice: x: 4, y: 4, z: 8, core: 2. Of those that a mesh axis runs over, the one named last changes fastest.
Arguments:
- gradient_rhs: float32 [2, 2048, 240], P(None, 'row'), may hold values from -6 to 6
- pivots: int32 [2048], replicated, may hold values from 0 to 2047, each once
- solved_prev: float32 [2, 131072, 240], P(None, 'row'), may hold values from -6 to 6
- upper_cols: float32 [2, 131072, 2, 1024], P(None, 'row', None, 'col'), may hold values from -0.01171875 to 0.01171875
- upper_coupling: float32 [2, 1024, 1024], P(None, 'row', 'col'), may hold values from -0.125 to 0.125
- block_inverse: float32 [2, 2, 1024, 1024], P(None, None, 'row', 'col'), may hold values from -0.125 to 0.125
Outputs:
- solution: float32 [2, 2, 1024, 240], P(None, None, 'row')
Inputs may be any that keep to these rules, and one draw needn't show every extreme that they name: pivots names each of the 2048 rows of gradient_rhs exactly once.
All inputs are finite; a program needn't handle non-finite values.
Results may differ from a plain program's by a relative error of at most 0.00008.
Values sent between devices are 32-bit elements; how exact they have to be, the bound alone decides.
No kernel may reach another device: no remote copies, remote signals or barrier semaphores. Data moves between devices by JAX's collectives and lax.ppermute only.
A program may use at most 64 MiB of HBM per device.

v0:
```python
import jax
import jax.numpy as jnp
from jax import lax
from jax.sharding import PartitionSpec as P

NB = 1024


HIGH = lax.Precision.HIGHEST


def contract(matrix, vector):
    return lax.dot_general(
        matrix, vector, (((0,), (0,)), ((), ())), precision=HIGH, preferred_element_type=jnp.float32
    )


def herm_product(upper_part, solved):
    real_part = contract(upper_part[0], solved[0]) + contract(upper_part[1], solved[1])
    imag_part = contract(upper_part[0], solved[1]) - contract(upper_part[1], solved[0])
    return jnp.stack([real_part, imag_part])


def apply_complex(matrix, vector):

    def mult(left, right):
        return jnp.dot(left, right, precision=HIGH, preferred_element_type=jnp.float32)

    real_part = mult(matrix[0], vector[0]) - mult(matrix[1], vector[1])
    imag_part = mult(matrix[0], vector[1]) + mult(matrix[1], vector[0])
    return jnp.stack([real_part, imag_part])


def on_device(gradient_rhs, pivots, solved_prev, upper_cols, upper_coupling, block_inverse):
    col_pos = lax.axis_index("col")
    col_width = upper_cols.shape[3]
    rhs_count = gradient_rhs.shape[2]

    def column_share(panel):
        return herm_product(upper_cols[:, :, panel, :], solved_prev)

    def target_rows(panel):
        return lax.dynamic_slice_in_dim(pivots, panel * NB + col_pos * col_width, col_width)

    gathered = lax.all_gather(gradient_rhs, "row", axis=1, tiled=True)

    def pivot_term():
        return jnp.zeros((2, col_width, rhs_count), jnp.float32)

    def pivot_known(panel):
        return jnp.take(gathered, target_rows(panel), axis=1)

    def solve_panel(panel, rhs_block):
        share = apply_complex(block_inverse[:, panel], rhs_block)
        return lax.psum(share, "col")

    def reduce_block(term):
        return lax.psum(term, "row")

    rhs_first = pivot_known(0) + reduce_block(pivot_term() - column_share(0))
    first_block = solve_panel(0, rhs_first)
    coupled = herm_product(upper_coupling, first_block)
    rhs_second = pivot_known(1) + reduce_block(pivot_term() - column_share(1) - coupled)
    second_block = solve_panel(1, rhs_second)
    return jnp.stack([first_block, second_block], axis=1)


def solution(mesh):
    placed = (
        P(None, "row", None),
        P(),
        P(None, "row", None),
        P(None, "row", None, "col"),
        P(None, "row", "col"),
        P(None, None, "row", "col"),
    )
    return jax.shard_map(
        on_device, mesh=mesh, in_specs=placed, out_specs=P(None, None, "row", None), check_vma=False
    )
```

profile of v0, /device:TPU:1, one launch (start us, length us, event | category | flops | bytes accessed | tf_op | source)
XLA Modules:
  0.0 355.2 jit_solution(14220060756831852947)
XLA Ops:
  6.5 1.7 copy.12
  8.2 0.0 all-gather.2.cloned.1.call-update
  8.2 0.0 all-reduce.3.cloned.1.call-start
  8.3 0.0 copy-start
  8.3 12.5 %fusion.85 = (f32[1,4096,1,128]{3,2,1,0:T(1,128)S(1)}, f32[1,4096,1,128]{3,2,1,0:T(1,128)S(1)}, f32[1,4096,1,128]{3,2,1,0:T(1,128)}, f32[1,4096,1,128]{3,2,1,0:T(1,128)S(1)}) fusion(f32[2,4096,2,128]{3,2,1,0:T(2,128)} %param.11), kind=kLoop, calls=%fused_computation.96 | loop fusion | bytes 16777216 | tf_op jit(solution)/shard_map/slice | solution.py:19
  20.7 5.3 %fusion.4 = f32[128,240]{0,1:T(8,128)S(1)} fusion(f32[4096,128]{1,0:T(8,128)S(1)} %bitcast.145, f32[2,4096,240]{1,2,0:T(8,128)} %param.10), kind=kOutput, calls=%fused_computation.6 | convolution fusion | flops 1509949440 | bytes 6152192 | tf_op jit(solution)/shard_map/dot_general | solution.py:13
  26.1 3.2 fusion.33
  29.4 3.2 fusion.6
  32.6 3.5 fusion.27
  36.2 0.7 maximum_subtract_fusion
  36.9 0.0 all-reduce.3.cloned.1.call-update
  36.9 0.0 all-reduce.5.cloned.1.call-start
  37.0 0.0 slice-start
  37.0 5.5 %fusion = f32[128,240]{0,1:T(8,128)S(1)} fusion(f32[4096,128]{1,0:T(8,128)S(1)} %bitcast.141, f32[2,4096,240]{1,2,0:T(8,128)} %param.10), kind=kOutput, calls=%fused_computation.2 | convolution fusion | flops 1509949440 | bytes 6152192 | tf_op jit(solution)/shard_map/dot_general | solution.py:13
  42.5 0.0 copy-done.1
  42.5 0.0 slice-start.1
  42.5 5.5 %fusion.2 = f32[128,240]{0,1:T(8,128)S(1)} fusion(f32[4096,128]{1,0:T(8,128)S(1)} %bitcast.143, f32[2,4096,240]{1,2,0:T(8,128)} %param.10), kind=kOutput, calls=%fused_computation.4 | convolution fusion | flops 1509949440 | bytes 6152192 | tf_op jit(solution)/shard_map/dot_general | solution.py:13
  48.0 5.7 %fusion.45 = f32[1,128,240]{1,2,0:T(8,128)S(1)} fusion(f32[128,240]{0,1:T(8,128)S(1)} %fusion, f32[4096,128]{1,0:T(8,128)S(1)} %bitcast.144, f32[2,4096,240]{1,2,0:T(8,128)} %param.10), kind=kOutput, calls=%fused_computation.33 | convolution fusion | flops 1509980160 | bytes 6275072 | tf_op jit(solution)/shard_map/dot_general | solution.py:13
  53.8 0.0 copy-start.2
  53.8 0.0 copy-start.3
  53.8 3.6 %fusion.39 = f32[1,128,240]{1,2,0:T(8,128)S(1)} fusion(f32[128,240]{0,1:T(8,128)S(1)} %fusion.2, f32[4096,128]{1,0:T(8,128)S(1)} %bitcast.142, f32[2,4096,240]{1,2,0:T(8,128)S(1)} %bitcast.140), kind=kOutput, calls=%fused_computation.31 | convolution fusion | flops 1509980160 | bytes 6275072 | tf_op jit(solution)/shard_map/dot_general | solution.py:13
  57.4 0.8 compare_and_fusion
  58.2 7.0 %all-gather.2.cloned.1.call-done = f32[2,2048,240]{2,0,1:T(2,128)} async-done(((f32[2,64,240]{2,0,1:T(2,128)}), f32[2,2048,240]{2,0,1:T(2,128)}) %all-gather.2.cloned.1.call-update) | async-done | bytes 3932176 | tf_op jit(solution)/shard_map/all_gather | solution.py:45
  65.3 3.1 gather_fusion
  68.4 0.1 copy.13
  68.5 110.3 %all-reduce.3.cloned.1.call-done = f32[2,128,240]{1,2,0:T(8,128)} async-done(((f32[2,128,240]{1,2,0:T(8,128)}), f32[2,128,240]{1,2,0:T(8,128)}) %all-reduce.3.cloned.1.call-update) | async-done | bytes 245776 | tf_op jit(solution)/shard_map/psum | solution.py:58
  178.8 1.0 bitcast_add_fusion.1
  179.8 0.3 fusion.56
  180.1 0.3 fusion.55
  180.5 0.3 fusion.52
  180.8 0.3 fusion.53
  181.1 23.7 %psum.29 = f32[2,32,240]{2,1,0:T(8,128)S(1)} all-reduce(f32[2,32,240]{2,1,0:T(8,128)S(1)} %pad_maximum_fusion.1), channel_id=1, replica_groups=mesh['row'=32,'col'=8] {'col'}, use_global_device_ids=true, to_apply=%region_1.3 | all-reduce | flops 15360 | bytes 122880 | tf_op jit(solution)/shard_map/psum | solution.py:55
  204.8 0.4 fusion.60
  205.2 0.4 fusion.59
  205.6 0.4 fusion.48
  206.0 0.4 fusion.49
  206.4 0.7 fusion.54
  207.1 0.0 all-reduce.5.cloned.1.call-update
  207.1 3.1 gather_fusion.1
  210.2 0.1 copy.14
  210.4 111.6 %all-reduce.5.cloned.1.call-done = f32[2,128,240]{1,2,0:T(8,128)} async-done(((f32[2,128,240]{1,2,0:T(8,128)}), f32[2,128,240]{1,2,0:T(8,128)}) %all-reduce.5.cloned.1.call-update) | async-done | bytes 245776 | tf_op jit(solution)/shard_map/psum | solution.py:58
  322.0 1.0 bitcast_add_fusion
  322.9 0.3 fusion.58
  323.3 0.3 fusion.57
  323.6 0.3 fusion.50
  323.9 0.3 fusion.51
  324.3 23.7 %psum.31 = f32[2,1,32,240]{3,2,0,1:T(8,128)S(1)} all-reduce(f32[2,1,32,240]{3,2,0,1:T(8,128)S(1)} %maximum_bitcast_fusion), channel_id=1, replica_groups=mesh['row'=32,'col'=8] {'col'}, use_global_device_ids=true, to_apply=%region_3.5 | all-reduce | flops 15360 | bytes 122880 | tf_op jit(solution)/shard_map/psum | solution.py:55
  348.0 0.7 copy.15
  (12 shorter events, 0.0 us)
Async XLA Ops:
  6.5 58.7 %all-gather.2.cloned.1.call-start = ((), (), s32[]{:S(2)}) async-start(), calls=%async_computation | async-start | bytes 4325376 | tf_op jit(solution)/shard_map/all_gather | solution.py:45
  8.2 170.6 %all-reduce.3.cloned.1.call-start = ((), (), s32[]{:S(2)}) async-start(), calls=%async_computation.1 | async-start | bytes 491520 | tf_op jit(solution)/shard_map/psum | solution.py:58
  8.3 17.8 %copy-start = (f32[2,4096,240]{1,2,0:T(8,128)S(1)}, f32[2,4096,240]{1,2,0:T(8,128)}, u32[]{:S(2)}) copy-start(f32[2,4096,240]{1,2,0:T(8,128)} %param.10) | copy-start | bytes 23592964
  36.9 285.1 %all-reduce.5.cloned.1.call-start = ((), (), s32[]{:S(2)}) async-start(), calls=%async_computation.2 | async-start | bytes 491520 | tf_op jit(solution)/shard_map/psum | solution.py:58
  37.0 5.5 %copy-start.1 = (f32[1,4096,1,128]{3,2,1,0:T(1,128)S(1)}, f32[1,4096,1,128]{3,2,1,0:T(1,128)}, u32[]{:S(2)}) copy-start(f32[1,4096,1,128]{3,2,1,0:T(1,128)} %get-tuple-element.12) | copy-start | bytes 6291460
  37.0 16.8 %slice-start = ((s8[7864320]{0:T(1024)(128)(4,1)}), s8[4194304]{0:T(1024)(128)(4,1)S(1)}, s32[]{:S(2)}) async-start(s8[7864320]{0:T(1024)(128)(4,1)} %bitcast.139), calls=%async_computation.3 | async-start | bytes 8388608
  42.5 11.3 %slice-start.1 = ((s8[7864320]{0:T(1024)(128)(4,1)}), s8[3670016]{0:T(1024)(128)(4,1)S(1)}, s32[]{:S(2)}) async-start(s8[7864320]{0:T(1024)(128)(4,1)} %bitcast.139), calls=%async_computation.4 | async-start | bytes 7340032
  53.8 126.0 %copy-start.2 = (f32[2,2,32,128]{3,2,1,0:T(8,128)S(1)}, f32[2,2,32,128]{3,2,1,0:T(8,128)}, u32[]{:S(2)}) copy-start(f32[2,2,32,128]{3,2,1,0:T(8,128)} %param.13) | copy-start | bytes 196612
  53.8 151.0 %copy-start.3 = (f32[2,32,128]{2,1,0:T(8,128)S(1)}, f32[2,32,128]{2,1,0:T(8,128)}, u32[]{:S(2)}) copy-start(f32[2,32,128]{2,1,0:T(8,128)} %param.12) | copy-start | bytes 98308
Sparse Core Ops, SparseCore 0:
  9.9 55.3 all-gather.1
  68.5 110.2 all-reduce.2
  207.3 114.6 all-reduce.4
where the time goes:
time: 362 us; the launch traced here: 355 us
  waiting for transfers between devices  229 us (63%)
  blocking collectives  47.3 us (13%)
  matrix products  39.9 us (11%)
  local copies, waits for them, and re-layouts  21.2 us (6%)
  between operations  13.4 us (4%)
  other arithmetic  4.24 us (1%)
    psum x2, waiting for transfers between devices, reduce_block(): return lax.psum(term, 'row')  222 us
    psum x2, blocking collectives, solve_panel(): return lax.psum(share, 'col')  47.3 us
    dot_general x12, matrix products, contract(): lax.dot_general(matrix, vector, (((0,), (0,)), ((), ())), precision=HIGH,...  37.2 us
    slice x1, local copies, waits for them, and re-layouts, herm_product(): upper_part[1]  12.5 us
  transfers between devices with their start and end apart: 3, of which 3 were waited for; matrix products, arithmetic and copies ran while one was open for 16% of the time, Pallas kernels for 0%

commit v1 on v0

v1 whole, which is shorter than its diff:
```python
import jax
import jax.numpy as jnp
from jax import lax
from jax.experimental import pallas as pl
from jax.experimental.pallas import tpu as pltpu
from jax.sharding import PartitionSpec as P

NB = 1024
RHS = 240
ROWS = 32
CHIPS = 16
COLS = 8
CW = NB // COLS
RW = NB // ROWS
RC = 8
GRAD_ROWS = 2 * NB // ROWS
DEPTH = 512

NN = (((1,), (0,)), ((), ()))
NT = (((1,), (1,)), ((), ()))
TN = (((0,), (0,)), ((), ()))
F32 = jnp.float32
BF16 = jnp.bfloat16


def split(x):
    high = x.astype(BF16)
    return high, (x - high.astype(F32)).astype(BF16)


def dot(left, right, dims):
    return lax.dot_general(left, right, dims, preferred_element_type=F32)


def dot_split(left, right, dims):
    lh, ll = split(left)
    rh, rl = split(right)
    return dot(lh, rh, dims) + (dot(lh, rl, dims) + dot(ll, rh, dims))


def sums_kernel(ids, solved, upper, grad, pivots, out, acc):
    step = pl.program_id(0)

    @pl.when(step == 0)
    def _():
        acc[...] = jnp.zeros_like(acc)

    xh, xl = split(solved[...].reshape(2 * RHS, DEPTH))
    for k in range(2):
        rows = pl.ds(k, DEPTH, stride=2)
        wh, wl = split(jnp.concatenate([upper[0, rows, :], upper[1, rows, :]], axis=1))
        acc[k] += dot(xh, wh, NN) + (dot(xh, wl, NN) + dot(xl, wh, NN))

    @pl.when(step == pl.num_programs(0) - 1)
    def _():
        out[RHS // RC :] = jnp.zeros((ROWS - RHS // RC, 2 * RC, 2 * CW), F32)
        first_row = ids[0] * GRAD_ROWS
        places = lax.broadcasted_iota(jnp.int32, (GRAD_ROWS, CW), 0) + first_row
        for k in range(2):
            target = pivots[pl.ds(k * COLS + ids[1], 1), :]
            chosen = jnp.where(places == target, 1.0, 0.0).astype(BF16)
            re_re, re_im = acc[k, :RHS, :CW], acc[k, :RHS, CW:]
            im_re, im_im = acc[k, RHS:, :CW], acc[k, RHS:, CW:]
            sums = (re_re + im_im, im_re - re_im)
            for c in range(2):
                rest = grad[c].T
                known = jnp.zeros((RHS, CW), F32)
                for _ in range(3):
                    part = rest.astype(BF16)
                    known = known + dot(part, chosen, NN)
                    rest = rest - part.astype(F32)
                term = known - sums[c]
                out[: RHS // RC, c * RC : (c + 1) * RC, k * CW : (k + 1) * CW] = term.reshape(
                    RHS // RC, RC, CW
                )


def column_terms(ids, solved_t, upper_rows, gradient_rhs, pivots):
    depth = solved_t.shape[2]
    return pl.pallas_call(
        sums_kernel,
        out_shape=jax.ShapeDtypeStruct((ROWS, 2 * RC, 2 * CW), F32),
        grid_spec=pltpu.PrefetchScalarGridSpec(
            num_scalar_prefetch=1,
            grid=(depth // DEPTH,),
            in_specs=[
                pl.BlockSpec((2, RHS, DEPTH), lambda s, ids: (0, 0, s)),
                pl.BlockSpec((2, 2 * DEPTH, CW), lambda s, ids: (0, s, 0)),
                pl.BlockSpec((2, GRAD_ROWS, RHS), lambda s, ids: (0, 0, 0)),
                pl.BlockSpec((2 * COLS, CW), lambda s, ids: (0, 0)),
            ],
            out_specs=pl.BlockSpec((ROWS, 2 * RC, 2 * CW), lambda s, ids: (0, 0, 0)),
            scratch_shapes=[pltpu.VMEM((2, 2 * RHS, 2 * CW), F32)],
        ),
        compiler_params=pltpu.CompilerParams(vmem_limit_bytes=40 * 2**20),
        cost_estimate=pl.CostEstimate(
            flops=3 * 8 * RHS * depth * 2 * CW,
            bytes_accessed=4 * (2 * RHS * depth + 4 * depth * CW),
            transcendentals=0,
        ),
        name="column_terms",
    )(ids, solved_t, upper_rows, gradient_rhs, pivots)


def complex_rows(x):
    return jnp.concatenate([x, jnp.concatenate([-x[RC:], x[:RC]], axis=0)], axis=1)


def pair(blocks, which):
    half = CHIPS * RW
    return jnp.concatenate(
        [blocks[:, which].reshape(half, CW), blocks[:, which + 1].reshape(half, CW)], axis=1
    )


def first_kernel(terms, own, other, copies, rhs_second):
    rhs = jnp.sum(terms[...], axis=0)
    rhs_second[...] = rhs[:, CW:]
    left = complex_rows(rhs[:, :CW])
    half = CHIPS * RW
    for at, blocks in enumerate((own, other)):
        share = dot_split(left, pair(blocks, 0), NT)
        for z in range(COLS):
            copies[z, :, at * half : (at + 1) * half] = share


def second_kernel(ids, shares, rhs_second, own, other, packed):
    half = CHIPS * RW
    first = jnp.sum(shares[...], axis=0)
    product = dot_split(first[:, :half], pair(own, 2), NN) + dot_split(
        first[:, half:], pair(other, 2), NN
    )
    coupled = jnp.concatenate(
        [product[:RC, :CW] + product[RC:, CW:], product[RC:, :CW] - product[:RC, CW:]], axis=0
    )
    left = complex_rows(rhs_second[...] - coupled)
    core = lax.rem(ids[0], 2)
    for at, blocks in enumerate((own, other)):
        second = dot_split(left, pair(blocks, 4), NT)
        place = core if at == 0 else 1 - core
        for q in range(CHIPS):
            one = slice(at * half + q * RW, at * half + (q + 1) * RW)
            two = slice(q * RW, (q + 1) * RW)
            packed[2 * q + place] = jnp.concatenate(
                [first[:RC, one], first[RC:, one], second[:RC, two], second[RC:, two]], axis=1
            )


def turn_kernel(packed, first, copies):
    turned = packed[...].reshape(ROWS * RC, 4 * RW).T
    first[...] = turned[: 2 * RW]
    for z in range(COLS):
        copies[z] = turned[2 * RW :]


def join_kernel(first, shares, out):
    second = jnp.sum(shares[...], axis=0)
    for c in range(2):
        out[c, 0] = first[c * RW : (c + 1) * RW, :RHS]
        out[c, 1] = second[c * RW : (c + 1) * RW, :RHS]


VMEM = pl.BlockSpec(memory_space=pltpu.VMEM)
SMEM = pl.BlockSpec(memory_space=pltpu.SMEM)


def local(kernel, ins, shapes, name):
    return pl.pallas_call(
        kernel,
        in_specs=ins,
        out_specs=[VMEM] * len(shapes),
        out_shape=[jax.ShapeDtypeStruct(s, F32) for s in shapes],
        compiler_params=pltpu.CompilerParams(vmem_limit_bytes=24 * 2**20),
        name=name,
    )


SAME_CORE = [[2 * q + c for q in range(CHIPS)] for c in range(2)]
OTHER_CORE = [(i, i ^ 1) for i in range(ROWS)]


def exchange(x, axis, groups=None):
    return lax.all_to_all(x, axis, 0, 0, axis_index_groups=groups, tiled=True)


def on_device(gradient_rhs, pivots, solved_prev, upper_cols, upper_coupling, block_inverse):
    row = lax.axis_index("row")
    ids = jnp.stack([row, lax.axis_index("col")]).astype(jnp.int32)

    mine = jnp.concatenate([block_inverse[:, 0], upper_coupling, block_inverse[:, 1]], axis=0)
    own = exchange(jnp.broadcast_to(mine[None], (CHIPS,) + mine.shape), "row", SAME_CORE)
    other = lax.ppermute(own, "row", OTHER_CORE)

    terms = column_terms(
        ids,
        jnp.swapaxes(solved_prev, 1, 2),
        upper_cols.reshape(2, -1, CW),
        gradient_rhs,
        pivots.reshape(2 * COLS, CW),
    )
    terms = exchange(terms, "row")
    copies, rhs_second = local(
        first_kernel, [VMEM] * 3, [(COLS, 2 * RC, NB), (2 * RC, CW)], "first_share"
    )(terms, own, other)
    shares = exchange(copies, "col")
    (packed,) = local(
        second_kernel, [SMEM] + [VMEM] * 4, [(ROWS, RC, 4 * RW)], "second_share"
    )(ids, shares, rhs_second, own, other)
    packed = exchange(packed, "row")
    first, copies = local(
        turn_kernel, [VMEM], [(2 * RW, ROWS * RC), (COLS, 2 * RW, ROWS * RC)], "turn"
    )(packed)
    shares = exchange(copies, "col")
    (solved,) = local(join_kernel, [VMEM] * 2, [(2, 2, RW, RHS)], "join")(first, shares)
    return solved


def solution(mesh):
    placed = (
        P(None, "row", None),
        P(),
        P(None, "row", None),
        P(None, "row", None, "col"),
        P(None, "row", "col"),
        P(None, None, "row", "col"),
    )
    return jax.shard_map(
        on_device, mesh=mesh, in_specs=placed, out_specs=P(None, None, "row", None), check_vma=False
    )
```

time: 362 us -> 124 us (0.34); the launches traced: 355 us -> 124 us
  waiting for transfers between devices: 229 us -> 0.01 us
  blocking collectives: 47.3 us -> 102 us
  matrix products: 39.9 us -> 0 us
  local copies, waits for them, and re-layouts: 21.2 us -> 4.21 us
  Pallas kernels: 0 us -> 14.5 us
  between operations: 13.4 us -> 0.06 us
    psum x2 -> x0, waiting for transfers between devices: 222 us -> none  [reduce_block(): return lax.psum(term, 'row')]
    all_to_all x0 -> x5, blocking collectives: none -> 102 us  [exchange(): return lax.all_to_all(x, axis, 0, 0, axis_index_groups=groups, tiled=True)]
    psum x2 -> x0, blocking collectives: 47.3 us -> none  [solve_panel(): return lax.psum(share, 'col')]
    dot_general x20 -> x0, matrix products: 39.9 us -> none  [the longest x12 37.2 us: contract(): lax.dot_general(matrix, vector, (((0,), (0,)), ((), ())), precision=HIGH,...]
    pallas_call x0 -> x5, Pallas kernels: none -> 14.5 us  [the longest x1 11.3 us: column_terms(): pl.pallas_call(sums_kernel, out_shape=jax.ShapeDtypeStruct((ROWS, 2 * RC,...]
    slice x1 -> x0, local copies, waits for them, and re-layouts: 12.5 us -> none  [herm_product(): upper_part[1]]
    all_gather x1 -> x0, waiting for transfers between devices: 7.05 us -> none  [on_device(): gathered = lax.all_gather(gradient_rhs, 'row', axis=1, tiled=True)]
    gather x4 -> x0, local copies, waits for them, and re-layouts: 6.41 us -> none  [pivot_known(): return jnp.take(gathered, target_rows(panel), axis=1)]
  transfers between devices with their start and end apart: 3 -> 1, of which waited for: 3 -> 0; matrix products, arithmetic and copies ran while one was open for 16% -> 0% of each run, Pallas kernels for 0% -> 9%
where the time goes in v1:
time: 124 us
  blocking collectives  102 us (82%)
  Pallas kernels  14.5 us (12%)
  local copies, waits for them, and re-layouts  4.21 us (3%)
  starting transfers between devices  2.02 us (2%)
    all_to_all x5, blocking collectives, exchange(): return lax.all_to_all(x, axis, 0, 0, axis_index_groups=groups, tiled=True)  102 us
    pallas_call x1, Pallas kernels, column_terms(): pl.pallas_call(sums_kernel, out_shape=jax.ShapeDtypeStruct((ROWS, 2 * RC,...  11.3 us
    unnamed x6, local copies, waits for them, and re-layouts  3.25 us
  transfers between devices with their start and end apart: 1, of which 0 were waited for; matrix products, arithmetic and copies ran while one was open for 0% of the time, Pallas kernels for 9%

profile of v1, /device:TPU:1, one launch (start us, length us, event | category | flops | bytes accessed | tf_op | source)
XLA Modules:
  0.0 123.7 jit_solution(8925662296883430301)
XLA Ops:
  0.0 0.8 slice_bitcast_fusion.1
  0.8 0.8 pad_maximum_fusion
  1.5 0.2 broadcast_in_dim.2
  1.7 0.0 copy-start.1
  1.7 0.0 copy-start.2
  1.8 29.0 %all_to_all.25.own = f32[16,6,32,128]{3,2,1,0:T(8,128)S(1)} all-to-all(f32[16,6,32,128]{3,2,1,0:T(8,128)S(1)} %broadcast_in_dim.2), channel_id=1, replica_groups={{0,16,32,48,64,80,96,112,128,144,160,176,192,208,224,240},{8,24,40,56,7..., dimensions={0} | all-to-all | bytes 3145728 | tf_op jit(solution)/shard_map/all_to_all | solution.py:183
  30.8 2.0 %collective-permute-start = (f32[16,6,32,128]{3,2,1,0:T(8,128)S(1)}, f32[16,6,32,128]{3,2,1,0:T(8,128)S(1)}, u32[]{:S(2)}, u32[]{:S(2)}) collective-permute-start(f32[16,6,32,128]{3,2,1,0:T(8,128)S(1)} %all_to_all.25.own), channel_id=1, source_target_pairs={{0,8},{8,0},{16,24},{24,16},{32,40},{40,32},{48,56},{56,48},{64,72... | collective-permute-start | bytes 4718600 | tf_op jit(solution)/shard_map/ppermute | solution.py:192
  32.8 0.1 pad_add_fusion.ids
  32.9 0.0 copy-done.1
  32.9 0.0 copy-done.2
  32.9 0.0 copy-start
  32.9 3.2 %copy-done = f32[2,4096,240]{1,2,0:T(8,128)S(1)} copy-done((f32[2,4096,240]{1,2,0:T(8,128)S(1)}, f32[2,4096,240]{1,2,0:T(8,128)}, u32[]{:S(2)}) %copy-start) | copy-done | bytes 7864344
  36.1 11.3 %column_terms.1 = f32[32,16,256]{2,1,0:T(8,128)S(1)} custom-call(s32[2]{0:T(128)S(1)} %pad_add_fusion.ids, f32[2,240,4096]{2,1,0:T(8,128)S(1)} %bitcast.11, f32[2,8192,128]{2,1,0:T(8,128)} %bitcast.13, f32[2,64,240]{2,1,0:T(8,128)S(1)} %copy-done.1, s32[16,128]{1,0:T(8,128)S(1)} %bitcast.12), custom_call_target="tpu_custom_call" | custom-call | flops 6039797760 | bytes 16252928 | tf_op jit(solution)/shard_map/column_terms/pallas_call | solution.py:80
  47.4 15.4 %all_to_all.26.terms = f32[32,16,256]{2,1,0:T(8,128)S(1)} all-to-all(f32[32,16,256]{2,1,0:T(8,128)S(1)} %column_terms.1), channel_id=1, replica_groups=mesh['row'=32,'col'=8] {'row'}, dimensions={0} | all-to-all | bytes 1048576 | tf_op jit(solution)/shard_map/all_to_all | solution.py:183
  62.9 0.0 collective-permute-done.other
  62.9 0.5 first_share.1
  63.4 26.0 %all_to_all.27.shares = f32[8,16,1024]{2,1,0:T(8,128)S(1)} all-to-all(f32[8,16,1024]{2,1,0:T(8,128)S(1)} %get-tuple-element.9), channel_id=1, replica_groups=mesh['row'=32,'col'=8] {'col'}, dimensions={0} | all-to-all | bytes 1048576 | tf_op jit(solution)/shard_map/all_to_all | solution.py:183
  89.4 1.8 %second_share.1 = f32[32,8,128]{2,1,0:T(8,128)S(1)} custom-call(s32[2]{0:T(128)S(1)} %pad_add_fusion.ids, f32[8,16,1024]{2,1,0:T(8,128)S(1)} %all_to_all.27.shares, f32[16,128]{1,0:T(8,128)S(1)} %get-tuple-element.10.rhs_second, f32[16,6,32,128]{3,2,1,0:T(8,128)S(1)} %all_to_all.25.own, f32[16,6,32,128]{3,2,1,0:T(8,128)S(1)} %collective-permute-done.other), custom_call_target="tpu_custom_call" | custom-call | tf_op jit(solution)/shard_map/second_share/pallas_call | solution.py:206
  91.3 11.3 %all_to_all.28.packed = f32[32,8,128]{2,1,0:T(8,128)S(1)} all-to-all(f32[32,8,128]{2,1,0:T(8,128)S(1)} %second_share.1), channel_id=1, replica_groups=mesh['row'=32,'col'=8] {'row'}, dimensions={0} | all-to-all | bytes 262144 | tf_op jit(solution)/shard_map/all_to_all | solution.py:183
  102.6 0.1 turn.1
  102.7 20.4 %all_to_all.29.shares = f32[8,64,256]{2,1,0:T(8,128)S(1)} all-to-all(f32[8,64,256]{2,1,0:T(8,128)S(1)} %get-tuple-element.12), channel_id=1, replica_groups=mesh['row'=32,'col'=8] {'col'}, dimensions={0} | all-to-all | bytes 1048576 | tf_op jit(solution)/shard_map/all_to_all | solution.py:183
  123.0 0.7 join.1
Async XLA Ops:
  1.7 31.1 %copy-start.1 = (f32[2,64,240]{2,1,0:T(8,128)S(1)}, f32[2,64,240]{2,1,0:T(8,128)}, u32[]{:S(2)}) copy-start(f32[2,64,240]{2,1,0:T(8,128)} %grad.1) | copy-start | bytes 368644
  1.7 31.1 %copy-start.2 = (s32[2048]{0:T(1024)S(1)}, s32[2048]{0:T(1024)}, u32[]{:S(2)}) copy-start(s32[2048]{0:T(1024)} %param.7) | copy-start | bytes 24580
  30.8 32.1 %collective-permute-start = (f32[16,6,32,128]{3,2,1,0:T(8,128)S(1)}, f32[16,6,32,128]{3,2,1,0:T(8,128)S(1)}, u32[]{:S(2)}, u32[]{:S(2)}) collective-permute-start(f32[16,6,32,128]{3,2,1,0:T(8,128)S(1)} %all_to_all.25.own), channel_id=1, source_target_pairs={{0,8},{8,0},{16,24},{24,16},{32,40},{40,32},{48,56},{56,48},{64,72... | collective-permute-start | bytes 4718600 | tf_op jit(solution)/shard_map/ppermute | solution.py:192
  32.9 3.2 %copy-start = (f32[2,4096,240]{1,2,0:T(8,128)S(1)}, f32[2,4096,240]{1,2,0:T(8,128)}, u32[]{:S(2)}) copy-start(f32[2,4096,240]{1,2,0:T(8,128)} %param.8) | copy-start | bytes 23592964

commit v2 on v1

v2 whole, which is shorter than its diff:
```python
import jax
import jax.numpy as jnp
from jax import lax
from jax.experimental import pallas as pl
from jax.experimental.pallas import tpu as pltpu
from jax.sharding import PartitionSpec as P

NB = 1024
RHS = 240
ROWS = 32
CHIPS = 16
COLS = 8
CW = NB // COLS
RW = NB // ROWS
RC = 8
GRAD_ROWS = 2 * NB // ROWS
DEPTH = 512
AHEAD = 3

NN = (((1,), (0,)), ((), ()))
NT = (((1,), (1,)), ((), ()))
TN = (((0,), (0,)), ((), ()))
F32 = jnp.float32
BF16 = jnp.bfloat16
VMEM = pl.BlockSpec(memory_space=pltpu.VMEM)
ANY = pl.BlockSpec(memory_space=pl.ANY)


def split(x):
    high = x.astype(BF16)
    return high, (x - high.astype(F32)).astype(BF16)


def dot(left, right, dims):
    return lax.dot_general(left, right, dims, preferred_element_type=F32)


def dot_split(left, right, dims):
    lh, ll = split(left)
    rh, rl = split(right)
    return dot(lh, rh, dims) + (dot(lh, rl, dims) + dot(ll, rh, dims))


def prepare_kernel(inverse, coupling, copies, arrived):
    loads = (
        pltpu.make_async_copy(inverse.at[:, 0], copies.at[0, pl.ds(0, 2)], arrived.at[0]),
        pltpu.make_async_copy(coupling, copies.at[0, pl.ds(2, 2)], arrived.at[1]),
    )
    for load in loads:
        load.start()
    for load in loads:
        load.wait()
    copies[1:] = jnp.broadcast_to(copies[0], (CHIPS - 1, 4, RW, CW))


def known_terms(grad, pivots, out):
    first_row = lax.axis_index("row") * GRAD_ROWS
    places = lax.broadcasted_iota(jnp.int32, (GRAD_ROWS, CW), 0) + first_row
    for k in range(2):
        target = pivots[pl.ds(k * COLS + lax.axis_index("col"), 1), :]
        chosen = jnp.where(places == target, 1.0, 0.0).astype(BF16)
        for c in range(2):
            rest = grad[c].T
            known = jnp.zeros((RHS, CW), F32)
            for _ in range(3):
                part = rest.astype(BF16)
                known = known + dot(part, chosen, NN)
                rest = rest - part.astype(F32)
            out[: RHS // RC, c * RC : (c + 1) * RC, k * CW : (k + 1) * CW] = known.reshape(
                RHS // RC, RC, CW
            )


def sums_kernel(solved, upper, grad, pivots, mine, theirs, vectors, blocks, acc, out, arrived):
    steps = solved.shape[2] // DEPTH

    def loads(s):
        cols, rows = pl.ds(s * DEPTH, DEPTH), pl.ds(s * 2 * DEPTH, 2 * DEPTH)
        return (
            pltpu.make_async_copy(
                solved.at[:, :, cols], vectors.at[:, :, cols], arrived.at[0, s]
            ),
            pltpu.make_async_copy(upper.at[:, rows, :], blocks.at[:, rows, :], arrived.at[1, s]),
        )

    for s in range(AHEAD):
        for load in loads(s):
            load.start()
    acc[...] = jnp.zeros_like(acc)
    out[RHS // RC :] = jnp.zeros((ROWS - RHS // RC, 2 * RC, 2 * CW), F32)
    known_terms(grad, pivots, out)
    for s in range(steps):
        for load in loads(s):
            load.wait()
        if s + AHEAD < steps:
            for load in loads(s + AHEAD):
                load.start()
        xh, xl = split(vectors[:, :, s * DEPTH : (s + 1) * DEPTH].reshape(2 * RHS, DEPTH))
        for k in range(2):
            rows = pl.ds(s * 2 * DEPTH + k, DEPTH, stride=2)
            wh, wl = split(jnp.concatenate([blocks[0, rows, :], blocks[1, rows, :]], axis=1))
            acc[k] += dot(xh, wh, NN) + (dot(xh, wl, NN) + dot(xl, wh, NN))

    for k in range(2):
        re_re, re_im = acc[k, :RHS, :CW], acc[k, :RHS, CW:]
        im_re, im_im = acc[k, RHS:, :CW], acc[k, RHS:, CW:]
        for c, sums in enumerate((re_re + im_im, im_re - re_im)):
            place = (
                slice(0, RHS // RC),
                slice(c * RC, (c + 1) * RC),
                slice(k * CW, (k + 1) * CW),
            )
            out[place] = out[place] - sums.reshape(RHS // RC, RC, CW)
    core = lax.rem(lax.axis_index("row"), 2)
    mine[...] = out[pl.ds(core * CHIPS, CHIPS)]
    theirs[...] = out[pl.ds((1 - core) * CHIPS, CHIPS)]


def column_terms(solved_t, upper_rows, gradient_rhs, pivots):
    depth = solved_t.shape[2]
    return pl.pallas_call(
        sums_kernel,
        out_shape=[jax.ShapeDtypeStruct((CHIPS, 2 * RC, 2 * CW), F32)] * 2,
        in_specs=[ANY, ANY, VMEM, VMEM],
        out_specs=[VMEM] * 2,
        scratch_shapes=[
            pltpu.VMEM((2, RHS, depth), F32),
            pltpu.VMEM((2, 2 * depth, CW), F32),
            pltpu.VMEM((2, 2 * RHS, 2 * CW), F32),
            pltpu.VMEM((ROWS, 2 * RC, 2 * CW), F32),
            pltpu.SemaphoreType.DMA((2, depth // DEPTH)),
        ],
        compiler_params=pltpu.CompilerParams(vmem_limit_bytes=56 * 2**20),
        cost_estimate=pl.CostEstimate(
            flops=3 * 8 * RHS * depth * 2 * CW,
            bytes_accessed=4 * (2 * RHS * depth + 4 * depth * CW),
            transcendentals=0,
        ),
        name="column_terms",
    )(solved_t, upper_rows, gradient_rhs, pivots)


def complex_rows(x):
    return jnp.concatenate([x, jnp.concatenate([-x[RC:], x[:RC]], axis=0)], axis=1)


def pair(blocks, which):
    half = CHIPS * RW
    return jnp.concatenate(
        [blocks[:, which].reshape(half, CW), blocks[:, which + 1].reshape(half, CW)], axis=1
    )


def first_kernel(terms, own, other, copies, rhs_second):
    rhs = jnp.sum(terms[...], axis=0)
    rhs_second[...] = rhs[:, CW:]
    left = complex_rows(rhs[:, :CW])
    half = CHIPS * RW
    for at, blocks in enumerate((own, other)):
        share = dot_split(left, pair(blocks, 0), NT)
        for z in range(COLS):
            copies[z, :, at * half : (at + 1) * half] = share


def coupling_kernel(shares, rhs_second, own, other, packed):
    half = CHIPS * RW
    first = jnp.sum(shares[...], axis=0)
    product = dot_split(first[:, :half], pair(own, 2), NN) + dot_split(
        first[:, half:], pair(other, 2), NN
    )
    coupled = jnp.concatenate(
        [product[:RC, :CW] + product[RC:, CW:], product[RC:, :CW] - product[:RC, CW:]], axis=0
    )
    packed[:, : 2 * RC] = jnp.broadcast_to(rhs_second[...] - coupled, (ROWS, 2 * RC, CW))
    core = lax.rem(lax.axis_index("row"), 2)
    for at in range(2):
        place = core if at == 0 else 1 - core
        for q in range(CHIPS):
            one = slice(at * half + q * RW, at * half + (q + 1) * RW)
            packed[2 * q + place, 2 * RC :] = jnp.concatenate(
                [first[:RC, one], first[RC:, one], jnp.zeros((RC, CW - 2 * RW), F32)], axis=1
            )


def second_kernel(packed, inverse, first, copies):
    def ordered(part):
        chunks = packed[:, part * RC : (part + 1) * RC].reshape(CHIPS, 2, RC, CW)
        return jnp.concatenate([chunks[:, h].reshape(CHIPS * RC, CW) for h in range(2)], axis=0)

    rhs = jnp.concatenate([ordered(0), ordered(1)], axis=1)
    real, imaginary = inverse[0, 1], inverse[1, 1]
    left = jnp.concatenate(
        [
            jnp.concatenate([real, -imaginary], axis=1),
            jnp.concatenate([imaginary, real], axis=1),
        ],
        axis=0,
    )
    share = dot_split(left, rhs, NT)
    for z in range(COLS):
        copies[z] = share
    first[...] = ordered(2).T[: 2 * RW]


def join_kernel(first, shares, out):
    second = jnp.sum(shares[...], axis=0)
    for c in range(2):
        out[c, 0] = first[c * RW : (c + 1) * RW, :RHS]
        out[c, 1] = second[c * RW : (c + 1) * RW, :RHS]


def local(kernel, ins, shapes, name, scratch=(), limit=24):
    return pl.pallas_call(
        kernel,
        in_specs=ins,
        out_specs=[VMEM] * len(shapes),
        out_shape=[jax.ShapeDtypeStruct(s, F32) for s in shapes],
        scratch_shapes=scratch,
        compiler_params=pltpu.CompilerParams(vmem_limit_bytes=limit * 2**20),
        name=name,
    )


SAME_CORE = [[2 * q + c for q in range(CHIPS)] for c in range(2)]
OTHER_CORE = [(i, i ^ 1) for i in range(ROWS)]


def exchange(x, axis, groups=None):
    return lax.all_to_all(x, axis, 0, 0, axis_index_groups=groups, tiled=True)


def on_device(gradient_rhs, pivots, solved_prev, upper_cols, upper_coupling, block_inverse):
    (copies,) = local(
        prepare_kernel,
        [ANY] * 2,
        [(CHIPS, 4, RW, CW)],
        "prepare",
        [pltpu.SemaphoreType.DMA((2,))],
        limit=56,
    )(block_inverse, upper_coupling)
    own = exchange(copies, "row", SAME_CORE)

    mine, theirs = column_terms(
        jnp.swapaxes(solved_prev, 1, 2),
        upper_cols.reshape(2, -1, CW),
        gradient_rhs,
        pivots.reshape(2 * COLS, CW),
    )
    terms = mine + lax.ppermute(theirs, "row", OTHER_CORE)
    own, terms = lax.optimization_barrier((own, terms))
    other = lax.ppermute(own, "row", OTHER_CORE)
    terms = exchange(terms, "row", SAME_CORE)
    copies, rhs_second = local(
        first_kernel, [VMEM] * 3, [(COLS, 2 * RC, NB), (2 * RC, CW)], "first_share"
    )(terms, own, other)
    shares = exchange(copies, "col")
    (packed,) = local(
        coupling_kernel, [VMEM] * 4, [(ROWS, 3 * RC, CW)], "coupling"
    )(shares, rhs_second, own, other)
    packed = exchange(packed, "row")
    first, copies = local(
        second_kernel, [VMEM] * 2, [(2 * RW, ROWS * RC), (COLS, 2 * RW, ROWS * RC)], "second_share"
    )(packed, block_inverse)
    shares = exchange(copies, "col")
    (solved,) = local(join_kernel, [VMEM] * 2, [(2, 2, RW, RHS)], "join")(first, shares)
    return solved


def solution(mesh):
    placed = (
        P(None, "row", None),
        P(),
        P(None, "row", None),
        P(None, "row", None, "col"),
        P(None, "row", "col"),
        P(None, None, "row", "col"),
    )
    return jax.shard_map(
        on_device, mesh=mesh, in_specs=placed, out_specs=P(None, None, "row", None), check_vma=False
    )
```

time: 124 us -> 102 us (0.82)
  blocking collectives: 102 us -> 71.8 us
  starting transfers between devices: 2.02 us -> 11.8 us
  local copies, waits for them, and re-layouts: 4.21 us -> 0.01 us
  waiting for transfers between devices: 0.01 us -> 3.24 us
    all_to_all x5 -> x4, blocking collectives: 102 us -> 71.8 us  [exchange(): return lax.all_to_all(x, axis, 0, 0, axis_index_groups=groups, tiled=True)]
    all_to_all x0 -> x1, starting transfers between devices: none -> 7.6 us  [exchange(): return lax.all_to_all(x, axis, 0, 0, axis_index_groups=groups, tiled=True)]
    unnamed x6 -> x2, local copies, waits for them, and re-layouts: 3.25 us -> 0.01 us
    all_to_all x0 -> x1, waiting for transfers between devices: none -> 1.87 us  [exchange(): return lax.all_to_all(x, axis, 0, 0, axis_index_groups=groups, tiled=True)]
    ppermute x0 -> x1, waiting for transfers between devices: none -> 1.37 us  [on_device(): terms = mine + lax.ppermute(theirs, 'row', OTHER_CORE)]
    pallas_call x3 -> x4, Pallas kernels: 13.3 us -> 12.8 us  [the longest x1 10.2 us: column_terms(): pl.pallas_call(sums_kernel, out_shape=[jax.ShapeDtypeStruct((CHIPS, 2 * R...]
  transfers between devices with their start and end apart: 1 -> 3, of which waited for: 0 -> 2; matrix products, arithmetic and copies ran while one was open for 0% -> 1% of each run, Pallas kernels for 9% -> 10%
where the time goes in v2:
time: 102 us
  blocking collectives  71.8 us (70%)
  Pallas kernels  14 us (14%)
  starting transfers between devices  11.8 us (12%)
  waiting for transfers between devices  3.24 us (3%)
    all_to_all x4, blocking collectives, exchange(): return lax.all_to_all(x, axis, 0, 0, axis_index_groups=groups, tiled=True)  71.8 us
    pallas_call x1, Pallas kernels, column_terms(): pl.pallas_call(sums_kernel, out_shape=[jax.ShapeDtypeStruct((CHIPS, 2 * R...  10.2 us
    all_to_all x1, starting transfers between devices, exchange(): return lax.all_to_all(x, axis, 0, 0, axis_index_groups=groups, tiled=True)  7.6 us
    ppermute x1, starting transfers between devices, on_device(): other = lax.ppermute(own, 'row', OTHER_CORE)  3.14 us
  transfers between devices with their start and end apart: 3, of which 2 were waited for; matrix products, arithmetic and copies ran while one was open for 1% of the time, Pallas kernels for 10%

profile of v2, /device:TPU:1, one launch (start us, length us, event | category | flops | bytes accessed | tf_op | source)
XLA Modules:
  0.0 101.9 jit_solution(17688898329710170484)
XLA Ops:
  0.0 1.9 %prepare.1 = f32[16,4,32,128]{3,2,1,0:T(8,128)} custom-call(f32[2,2,32,128]{3,2,1,0:T(8,128)} %inverse.3, f32[2,32,128]{2,1,0:T(8,128)} %coupling.2), custom_call_target="tpu_custom_call" | custom-call | tf_op jit(solution)/shard_map/prepare/pallas_call | solution.py:233
  1.9 7.6 %all-to-all-start = ((f32[16,4,32,128]{3,2,1,0:T(8,128)}), f32[16,4,32,128]{3,2,1,0:T(8,128)S(1)}, u32[]{:S(2)}, u32[]{:S(2)}) async-start(f32[16,4,32,128]{3,2,1,0:T(8,128)} %prepare.1), calls=%async_computation | async-start | bytes 2097152 | tf_op jit(solution)/shard_map/all_to_all | solution.py:229
  9.5 10.2 %column_terms.1 = (f32[16,16,256]{2,1,0:T(8,128)}, f32[16,16,256]{2,1,0:T(8,128)}) custom-call(f32[2,240,4096]{2,1,0:T(8,128)} %bitcast.4, f32[2,8192,128]{2,1,0:T(8,128)} %bitcast.3, f32[2,64,240]{2,1,0:T(8,128)} %grad.1, s32[16,128]{1,0:T(8,128)} %bitcast.5), custom_call_target="tpu_custom_call" | custom-call | flops 6039797760 | bytes 16252928 | tf_op jit(solution)/shard_map/column_terms/pallas_call | solution.py:121
  19.7 0.0 copy-start
  19.7 1.0 %collective-permute-start = (f32[16,16,256]{2,1,0:T(8,128)}, f32[16,16,256]{2,1,0:T(8,128)S(1)}, u32[]{:S(2)}, u32[]{:S(2)}) collective-permute-start(f32[16,16,256]{2,1,0:T(8,128)} %get-tuple-element.14), channel_id=1, source_target_pairs={{0,8},{8,0},{16,24},{24,16},{32,40},{40,32},{48,56},{56,48},{64,72... | collective-permute-start | bytes 786440 | tf_op jit(solution)/shard_map/ppermute | solution.py:249
  20.7 1.4 %collective-permute-done = f32[16,16,256]{2,1,0:T(8,128)S(1)} collective-permute-done((f32[16,16,256]{2,1,0:T(8,128)}, f32[16,16,256]{2,1,0:T(8,128)S(1)}, u32[]{:S(2)}, u32[]{:S(2)}) %collective-permute-start) | collective-permute-done | bytes 262176 | tf_op jit(solution)/shard_map/ppermute | solution.py:249
  22.1 1.0 add.3
  23.1 1.9 %all-to-all-done.own = f32[16,4,32,128]{3,2,1,0:T(8,128)S(1)} async-done(((f32[16,4,32,128]{3,2,1,0:T(8,128)}), f32[16,4,32,128]{3,2,1,0:T(8,128)S(1)}, u32[]{:S(2)}, u32[]{:S(2)}) %all-to-all-start) | async-done | bytes 1048608 | tf_op jit(solution)/shard_map/all_to_all | solution.py:229
  25.0 3.1 %collective-permute-start.1 = (f32[16,4,32,128]{3,2,1,0:T(8,128)S(1)}, f32[16,4,32,128]{3,2,1,0:T(8,128)S(1)}, u32[]{:S(2)}, u32[]{:S(2)}) collective-permute-start(f32[16,4,32,128]{3,2,1,0:T(8,128)S(1)} %all-to-all-done.own), channel_id=1, source_target_pairs={{0,8},{8,0},{16,24},{24,16},{32,40},{40,32},{48,56},{56,48},{64,72... | collective-permute-start | bytes 3145736 | tf_op jit(solution)/shard_map/ppermute | solution.py:251
  28.1 10.6 %all_to_all.25.terms = f32[16,16,256]{2,1,0:T(8,128)S(1)} all-to-all(f32[16,16,256]{2,1,0:T(8,128)S(1)} %add.3), channel_id=1, replica_groups={{0,16,32,48,64,80,96,112,128,144,160,176,192,208,224,240},{8,24,40,56,7..., dimensions={0} | all-to-all | bytes 524288 | tf_op jit(solution)/shard_map/all_to_all | solution.py:229
  38.7 0.0 collective-permute-done.1.other
  38.7 0.6 first_share.1
  39.3 22.7 %all_to_all.26.shares = f32[8,16,1024]{2,1,0:T(8,128)S(1)} all-to-all(f32[8,16,1024]{2,1,0:T(8,128)S(1)} %get-tuple-element.17), channel_id=1, replica_groups=mesh['row'=32,'col'=8] {'col'}, dimensions={0} | all-to-all | bytes 1048576 | tf_op jit(solution)/shard_map/all_to_all | solution.py:229
  62.0 0.4 coupling.3
  62.4 18.1 %all_to_all.27.packed = f32[32,24,128]{2,1,0:T(8,128)S(1)} all-to-all(f32[32,24,128]{2,1,0:T(8,128)S(1)} %coupling.3), channel_id=1, replica_groups=mesh['row'=32,'col'=8] {'row'}, dimensions={0} | all-to-all | bytes 786432 | tf_op jit(solution)/shard_map/all_to_all | solution.py:229
  80.4 0.0 copy-done
  80.4 0.3 second_share.1
  80.7 20.4 %all_to_all.28.shares = f32[8,64,256]{2,1,0:T(8,128)S(1)} all-to-all(f32[8,64,256]{2,1,0:T(8,128)S(1)} %get-tuple-element.20), channel_id=1, replica_groups=mesh['row'=32,'col'=8] {'col'}, dimensions={0} | all-to-all | bytes 1048576 | tf_op jit(solution)/shard_map/all_to_all | solution.py:229
  101.2 0.7 join.1
Async XLA Ops:
  1.9 23.1 %all-to-all-start = ((f32[16,4,32,128]{3,2,1,0:T(8,128)}), f32[16,4,32,128]{3,2,1,0:T(8,128)S(1)}, u32[]{:S(2)}, u32[]{:S(2)}) async-start(f32[16,4,32,128]{3,2,1,0:T(8,128)} %prepare.1), calls=%async_computation | async-start | bytes 2097152 | tf_op jit(solution)/shard_map/all_to_all | solution.py:229
  19.7 60.8 %copy-start = (f32[2,2,32,128]{3,2,1,0:T(8,128)S(1)}, f32[2,2,32,128]{3,2,1,0:T(8,128)}, u32[]{:S(2)}) copy-start(f32[2,2,32,128]{3,2,1,0:T(8,128)} %inverse.3) | copy-start | bytes 196612
  19.7 2.4 %collective-permute-start = (f32[16,16,256]{2,1,0:T(8,128)}, f32[16,16,256]{2,1,0:T(8,128)S(1)}, u32[]{:S(2)}, u32[]{:S(2)}) collective-permute-start(f32[16,16,256]{2,1,0:T(8,128)} %get-tuple-element.14), channel_id=1, source_target_pairs={{0,8},{8,0},{16,24},{24,16},{32,40},{40,32},{48,56},{56,48},{64,72... | collective-permute-start | bytes 786440 | tf_op jit(solution)/shard_map/ppermute | solution.py:249
  25.0 13.8 %collective-permute-start.1 = (f32[16,4,32,128]{3,2,1,0:T(8,128)S(1)}, f32[16,4,32,128]{3,2,1,0:T(8,128)S(1)}, u32[]{:S(2)}, u32[]{:S(2)}) collective-permute-start(f32[16,4,32,128]{3,2,1,0:T(8,128)S(1)} %all-to-all-done.own), channel_id=1, source_target_pairs={{0,8},{8,0},{16,24},{24,16},{32,40},{40,32},{48,56},{56,48},{64,72... | collective-permute-start | bytes 3145736 | tf_op jit(solution)/shard_map/ppermute | solution.py:251

commit v3 on v2

--- a/solution.py
+++ b/solution.py
@@ -23,7 +23,7 @@
 F32 = jnp.float32
 BF16 = jnp.bfloat16
 VMEM = pl.BlockSpec(memory_space=pltpu.VMEM)
-ANY = pl.BlockSpec(memory_space=pl.ANY)
+HBM = pl.BlockSpec(memory_space=pl.ANY)
 
 
 def split(x):
@@ -41,19 +41,23 @@
     return dot(lh, rh, dims) + (dot(lh, rl, dims) + dot(ll, rh, dims))
 
 
-def prepare_kernel(inverse, coupling, copies, arrived):
+def prepare_kernel(inverse, coupling, copies, mine, arrived, sent):
     loads = (
-        pltpu.make_async_copy(inverse.at[:, 0], copies.at[0, pl.ds(0, 2)], arrived.at[0]),
-        pltpu.make_async_copy(coupling, copies.at[0, pl.ds(2, 2)], arrived.at[1]),
+        pltpu.make_async_copy(inverse.at[:, 0], mine.at[pl.ds(0, 2)], arrived.at[0]),
+        pltpu.make_async_copy(coupling, mine.at[pl.ds(2, 2)], arrived.at[1]),
     )
     for load in loads:
         load.start()
     for load in loads:
         load.wait()
-    copies[1:] = jnp.broadcast_to(copies[0], (CHIPS - 1, 4, RW, CW))
-
-
-def known_terms(grad, pivots, out):
+    stores = [pltpu.make_async_copy(mine, copies.at[q], sent.at[q]) for q in range(CHIPS)]
+    for store in stores:
+        store.start()
+    for store in stores:
+        store.wait()
+
+
+def known_terms(grad, pivots, known):
     first_row = lax.axis_index("row") * GRAD_ROWS
     places = lax.broadcasted_iota(jnp.int32, (GRAD_ROWS, CW), 0) + first_row
     for k in range(2):
@@ -61,17 +65,19 @@
         chosen = jnp.where(places == target, 1.0, 0.0).astype(BF16)
         for c in range(2):
             rest = grad[c].T
-            known = jnp.zeros((RHS, CW), F32)
+            rows = jnp.zeros((RHS, CW), F32)
             for _ in range(3):
                 part = rest.astype(BF16)
-                known = known + dot(part, chosen, NN)
+                rows = rows + dot(part, chosen, NN)
                 rest = rest - part.astype(F32)
-            out[: RHS // RC, c * RC : (c + 1) * RC, k * CW : (k + 1) * CW] = known.reshape(
+            known[:, c * RC : (c + 1) * RC, k * CW : (k + 1) * CW] = rows.reshape(
                 RHS // RC, RC, CW
             )
 
 
-def sums_kernel(solved, upper, grad, pivots, mine, theirs, vectors, blocks, acc, out, arrived):
+def sums_kernel(
+    solved, upper, gradient_rhs, all_pivots, mine, theirs, vectors, blocks, grad, pivots, acc, known, arrived
+):
     steps = solved.shape[2] // DEPTH
 
     def loads(s):
@@ -83,12 +89,18 @@
             pltpu.make_async_copy(upper.at[:, rows, :], blocks.at[:, rows, :], arrived.at[1, s]),
         )
 
+    small = (
+        pltpu.make_async_copy(gradient_rhs, grad, arrived.at[0, steps]),
+        pltpu.make_async_copy(all_pivots, pivots, arrived.at[1, steps]),
+    )
+    for load in small:
+        load.start()
     for s in range(AHEAD):
         for load in loads(s):
             load.start()
-    acc[...] = jnp.zeros_like(acc)
-    out[RHS // RC :] = jnp.zeros((ROWS - RHS // RC, 2 * RC, 2 * CW), F32)
-    known_terms(grad, pivots, out)
+    for load in small:
+        load.wait()
+    known_terms(grad, pivots, known)
     for s in range(steps):
         for load in loads(s):
             load.wait()
@@ -99,21 +111,33 @@
         for k in range(2):
             rows = pl.ds(s * 2 * DEPTH + k, DEPTH, stride=2)
             wh, wl = split(jnp.concatenate([blocks[0, rows, :], blocks[1, rows, :]], axis=1))
-            acc[k] += dot(xh, wh, NN) + (dot(xh, wl, NN) + dot(xl, wh, NN))
-
-    for k in range(2):
-        re_re, re_im = acc[k, :RHS, :CW], acc[k, :RHS, CW:]
-        im_re, im_im = acc[k, RHS:, :CW], acc[k, RHS:, CW:]
-        for c, sums in enumerate((re_re + im_im, im_re - re_im)):
-            place = (
-                slice(0, RHS // RC),
-                slice(c * RC, (c + 1) * RC),
-                slice(k * CW, (k + 1) * CW),
+            product = dot(xh, wh, NN) + (dot(xh, wl, NN) + dot(xl, wh, NN))
+            acc[k] = product if s == 0 else acc[k] + product
+
+    def close(half, to):
+        first, last = half * CHIPS * RC, min((half + 1) * CHIPS * RC, RHS)
+        chunks = (last - first) // RC
+        for k in range(2):
+            panel = slice(k * CW, (k + 1) * CW)
+            re_re, re_im = (acc[k, first:last, at * CW : (at + 1) * CW] for at in range(2))
+            im_re, im_im = (
+                acc[k, RHS + first : RHS + last, at * CW : (at + 1) * CW] for at in range(2)
             )
-            out[place] = out[place] - sums.reshape(RHS // RC, RC, CW)
+            for c, sums in enumerate((re_re + im_im, im_re - re_im)):
+                rows = slice(c * RC, (c + 1) * RC)
+                to[:chunks, rows, panel] = known[
+                    first // RC : last // RC, rows, panel
+                ] - sums.reshape(chunks, RC, CW)
+        if chunks < CHIPS:
+            to[chunks:] = jnp.zeros((CHIPS - chunks, 2 * RC, 2 * CW), F32)
+
     core = lax.rem(lax.axis_index("row"), 2)
-    mine[...] = out[pl.ds(core * CHIPS, CHIPS)]
-    theirs[...] = out[pl.ds((1 - core) * CHIPS, CHIPS)]
+    for half in range(2):
+
+        @pl.when(core == half)
+        def _():
+            close(half, mine)
+            close(1 - half, theirs)
 
 
 def column_terms(solved_t, upper_rows, gradient_rhs, pivots):
@@ -121,16 +145,18 @@
     return pl.pallas_call(
         sums_kernel,
         out_shape=[jax.ShapeDtypeStruct((CHIPS, 2 * RC, 2 * CW), F32)] * 2,
-        in_specs=[ANY, ANY, VMEM, VMEM],
+        in_specs=[HBM] * 4,
         out_specs=[VMEM] * 2,
         scratch_shapes=[
             pltpu.VMEM((2, RHS, depth), F32),
             pltpu.VMEM((2, 2 * depth, CW), F32),
+            pltpu.VMEM((2, GRAD_ROWS, RHS), F32),
+            pltpu.VMEM((2 * COLS, CW), jnp.int32),
             pltpu.VMEM((2, 2 * RHS, 2 * CW), F32),
-            pltpu.VMEM((ROWS, 2 * RC, 2 * CW), F32),
-            pltpu.SemaphoreType.DMA((2, depth // DEPTH)),
+            pltpu.VMEM((RHS // RC, 2 * RC, 2 * CW), F32),
+            pltpu.SemaphoreType.DMA((2, depth // DEPTH + 1)),
         ],
-        compiler_params=pltpu.CompilerParams(vmem_limit_bytes=56 * 2**20),
+        compiler_params=pltpu.CompilerParams(vmem_limit_bytes=50 * 2**20),
         cost_estimate=pl.CostEstimate(
             flops=3 * 8 * RHS * depth * 2 * CW,
             bytes_accessed=4 * (2 * RHS * depth + 4 * depth * CW),
@@ -171,23 +197,16 @@
     coupled = jnp.concatenate(
         [product[:RC, :CW] + product[RC:, CW:], product[RC:, :CW] - product[:RC, CW:]], axis=0
     )
-    packed[:, : 2 * RC] = jnp.broadcast_to(rhs_second[...] - coupled, (ROWS, 2 * RC, CW))
-    core = lax.rem(lax.axis_index("row"), 2)
-    for at in range(2):
-        place = core if at == 0 else 1 - core
-        for q in range(CHIPS):
-            one = slice(at * half + q * RW, at * half + (q + 1) * RW)
-            packed[2 * q + place, 2 * RC :] = jnp.concatenate(
-                [first[:RC, one], first[RC:, one], jnp.zeros((RC, CW - 2 * RW), F32)], axis=1
-            )
-
-
-def second_kernel(packed, inverse, first, copies):
-    def ordered(part):
-        chunks = packed[:, part * RC : (part + 1) * RC].reshape(CHIPS, 2, RC, CW)
-        return jnp.concatenate([chunks[:, h].reshape(CHIPS * RC, CW) for h in range(2)], axis=0)
-
-    rhs = jnp.concatenate([ordered(0), ordered(1)], axis=1)
+    packed[:, : 2 * RC] = jnp.broadcast_to(rhs_second[...] - coupled, (CHIPS, 2 * RC, CW))
+    for q in range(CHIPS):
+        one = slice(q * RW, (q + 1) * RW)
+        two = slice(half + q * RW, half + (q + 1) * RW)
+        packed[q, 2 * RC :] = jnp.concatenate(
+            [first[:RC, one], first[RC:, one], first[:RC, two], first[RC:, two]], axis=1
+        )
+
+
+def second_kernel(mine, theirs, inverse, first, copies):
     real, imaginary = inverse[0, 1], inverse[1, 1]
     left = jnp.concatenate(
         [
@@ -196,10 +215,18 @@
         ],
         axis=0,
     )
-    share = dot_split(left, rhs, NT)
-    for z in range(COLS):
-        copies[z] = share
-    first[...] = ordered(2).T[: 2 * RW]
+    shares, rows = [], []
+    for at, got in enumerate((mine, theirs)):
+        parts = [got[:, p * RC : (p + 1) * RC].reshape(CHIPS * RC, CW) for p in range(3)]
+        shares.append(dot_split(left, jnp.concatenate(parts[:2], axis=1), NT))
+        rows.append(parts[2].T[at * 2 * RW : (at + 1) * 2 * RW])
+    core = lax.rem(lax.axis_index("row"), 2)
+    for half in range(2):
+        place = slice(half * CHIPS * RC, (half + 1) * CHIPS * RC)
+        first[:, place] = jnp.where(core == half, rows[0], rows[1])
+        share = jnp.where(core == half, shares[0], shares[1])
+        for z in range(COLS):
+            copies[z, :, place] = share
 
 
 def join_kernel(first, shares, out):
@@ -230,13 +257,19 @@
 
 
 def on_device(gradient_rhs, pivots, solved_prev, upper_cols, upper_coupling, block_inverse):
-    (copies,) = local(
+    copies = pl.pallas_call(
         prepare_kernel,
-        [ANY] * 2,
-        [(CHIPS, 4, RW, CW)],
-        "prepare",
-        [pltpu.SemaphoreType.DMA((2,))],
-        limit=56,
+        in_specs=[HBM] * 2,
+        out_specs=HBM,
+        out_shape=jax.ShapeDtypeStruct((CHIPS, 4, RW, CW), F32),
+        scratch_shapes=[
+            pltpu.VMEM((4, RW, CW), F32),
+            pltpu.SemaphoreType.DMA((2,)),
+            pltpu.SemaphoreType.DMA((CHIPS,)),
+        ],
+        compiler_params=pltpu.CompilerParams(vmem_limit_bytes=56 * 2**20),
+        cost_estimate=pl.CostEstimate(flops=10**10, bytes_accessed=2**25, transcendentals=0),
+        name="prepare",
     )(block_inverse, upper_coupling)
     own = exchange(copies, "row", SAME_CORE)
 
@@ -255,12 +288,13 @@
     )(terms, own, other)
     shares = exchange(copies, "col")
     (packed,) = local(
-        coupling_kernel, [VMEM] * 4, [(ROWS, 3 * RC, CW)], "coupling"
+        coupling_kernel, [VMEM] * 4, [(CHIPS, 3 * RC, CW)], "coupling"
     )(shares, rhs_second, own, other)
-    packed = exchange(packed, "row")
+    mine = exchange(packed, "row", SAME_CORE)
+    theirs = lax.ppermute(mine, "row", OTHER_CORE)
     first, copies = local(
-        second_kernel, [VMEM] * 2, [(2 * RW, ROWS * RC), (COLS, 2 * RW, ROWS * RC)], "second_share"
-    )(packed, block_inverse)
+        second_kernel, [VMEM] * 3, [(2 * RW, ROWS * RC), (COLS, 2 * RW, ROWS * RC)], "second_share"
+    )(mine, theirs, block_inverse)
     shares = exchange(copies, "col")
     (solved,) = local(join_kernel, [VMEM] * 2, [(2, 2, RW, RHS)], "join")(first, shares)
     return solved

time: 102 us -> 101 us (level)
  blocking collectives: 71.8 us -> 65 us
  starting transfers between devices: 11.8 us -> 16.2 us
  waiting for transfers between devices: 3.24 us -> 6.78 us
  Pallas kernels: 14 us -> 12.5 us
    all_to_all x4, blocking collectives: 71.8 us -> 65 us  [exchange(): return lax.all_to_all(x, axis, 0, 0, axis_index_groups=groups, tiled=True)]
    ppermute x0 -> x1, starting transfers between devices: none -> 4.42 us  [on_device(): theirs = lax.ppermute(mine, 'row', OTHER_CORE)]
    all_to_all x1, waiting for transfers between devices: 1.87 us -> 4.55 us  [exchange(): return lax.all_to_all(x, axis, 0, 0, axis_index_groups=groups, tiled=True)]
    pallas_call x1, Pallas kernels: 10.2 us -> 8.69 us  [column_terms(): pl.pallas_call(sums_kernel, out_shape=[jax.ShapeDtypeStruct((CHIPS, 2 * R...]
    ppermute x0 -> x1, waiting for transfers between devices: none -> 1.07 us  [on_device(): theirs = lax.ppermute(mine, 'row', OTHER_CORE)]
  transfers between devices with their start and end apart: 3 -> 4, of which waited for: 2 -> 3; matrix products, arithmetic and copies ran while one was open for 1% -> 0% of each run, Pallas kernels for 10% -> 9%
where the time goes in v3:
time: 101 us
  blocking collectives  65 us (64%)
  starting transfers between devices  16.2 us (16%)
  Pallas kernels  12.5 us (12%)
  waiting for transfers between devices  6.78 us (7%)
    all_to_all x4, blocking collectives, exchange(): return lax.all_to_all(x, axis, 0, 0, axis_index_groups=groups, tiled=True)  65 us
    pallas_call x1, Pallas kernels, column_terms(): pl.pallas_call(sums_kernel, out_shape=[jax.ShapeDtypeStruct((CHIPS, 2 * R...  8.69 us
    all_to_all x1, starting transfers between devices, exchange(): return lax.all_to_all(x, axis, 0, 0, axis_index_groups=groups, tiled=True)  7.6 us
    all_to_all x1, waiting for transfers between devices, exchange(): return lax.all_to_all(x, axis, 0, 0, axis_index_groups=groups, tiled=True)  4.55 us
    ppermute x1, starting transfers between devices, on_device(): theirs = lax.ppermute(mine, 'row', OTHER_CORE)  4.42 us
    ppermute x1, starting transfers between devices, on_device(): other = lax.ppermute(own, 'row', OTHER_CORE)  3.14 us
  transfers between devices with their start and end apart: 4, of which 3 were waited for; matrix products, arithmetic and copies ran while one was open for 0% of the time, Pallas kernels for 9%

profile of v3, /device:TPU:1, one launch (start us, length us, event | category | flops | bytes accessed | tf_op | source)
XLA Modules:
  0.0 100.7 jit_solution(5186140507047954260)
XLA Ops:
  0.0 0.0 copy-start.2
  0.0 0.0 copy-start.1
  0.0 1.9 %prepare.1 = f32[16,4,32,128]{3,2,1,0:T(8,128)} custom-call(f32[2,2,32,128]{3,2,1,0:T(8,128)} %inverse.3, f32[2,32,128]{2,1,0:T(8,128)} %coupling.2), custom_call_target="tpu_custom_call" | custom-call | flops 10000000000 | bytes 33554432 | tf_op jit(solution)/shard_map/prepare/pallas_call | solution.py:260
  2.0 7.6 %all-to-all-start = ((f32[16,4,32,128]{3,2,1,0:T(8,128)}), f32[16,4,32,128]{3,2,1,0:T(8,128)S(1)}, u32[]{:S(2)}, u32[]{:S(2)}) async-start(f32[16,4,32,128]{3,2,1,0:T(8,128)} %prepare.1), calls=%async_computation | async-start | bytes 2097152 | tf_op jit(solution)/shard_map/all_to_all | solution.py:256
  9.6 0.0 copy-done.2
  9.6 0.0 copy-done.1
  9.6 0.0 copy-start
  9.6 8.7 %column_terms.1 = (f32[16,16,256]{2,1,0:T(8,128)S(1)}, f32[16,16,256]{2,1,0:T(8,128)S(1)}) custom-call(f32[2,240,4096]{2,1,0:T(8,128)} %bitcast.5, f32[2,8192,128]{2,1,0:T(8,128)} %bitcast.4, f32[2,64,240]{2,1,0:T(8,128)S(1)} %copy-done.1, s32[16,128]{1,0:T(8,128)S(1)} %bitcast.3), custom_call_target="tpu_custom_call" | custom-call | flops 6039797760 | bytes 16252928 | tf_op jit(solution)/shard_map/column_terms/pallas_call | solution.py:145
  18.3 1.0 %collective-permute-start = (f32[16,16,256]{2,1,0:T(8,128)S(1)}, f32[16,16,256]{2,1,0:T(8,128)S(1)}, u32[]{:S(2)}, u32[]{:S(2)}) collective-permute-start(f32[16,16,256]{2,1,0:T(8,128)S(1)} %get-tuple-element.14), channel_id=1, source_target_pairs={{0,8},{8,0},{16,24},{24,16},{32,40},{40,32},{48,56},{56,48},{64,72... | collective-permute-start | bytes 786440 | tf_op jit(solution)/shard_map/ppermute | solution.py:282
  19.3 1.2 %collective-permute-done = f32[16,16,256]{2,1,0:T(8,128)S(1)} collective-permute-done((f32[16,16,256]{2,1,0:T(8,128)S(1)}, f32[16,16,256]{2,1,0:T(8,128)S(1)}, u32[]{:S(2)}, u32[]{:S(2)}) %collective-permute-start) | collective-permute-done | bytes 262176 | tf_op jit(solution)/shard_map/ppermute | solution.py:282
  20.5 4.5 %all-to-all-done.own = f32[16,4,32,128]{3,2,1,0:T(8,128)S(1)} async-done(((f32[16,4,32,128]{3,2,1,0:T(8,128)}), f32[16,4,32,128]{3,2,1,0:T(8,128)S(1)}, u32[]{:S(2)}, u32[]{:S(2)}) %all-to-all-start) | async-done | bytes 1048608 | tf_op jit(solution)/shard_map/all_to_all | solution.py:256
  25.1 3.1 %collective-permute-start.1 = (f32[16,4,32,128]{3,2,1,0:T(8,128)S(1)}, f32[16,4,32,128]{3,2,1,0:T(8,128)S(1)}, u32[]{:S(2)}, u32[]{:S(2)}) collective-permute-start(f32[16,4,32,128]{3,2,1,0:T(8,128)S(1)} %all-to-all-done.own), channel_id=1, source_target_pairs={{0,8},{8,0},{16,24},{24,16},{32,40},{40,32},{48,56},{56,48},{64,72... | collective-permute-start | bytes 3145736 | tf_op jit(solution)/shard_map/ppermute | solution.py:284
  28.2 10.6 %all_to_all.25.terms = f32[16,16,256]{2,1,0:T(8,128)S(1)} all-to-all(f32[16,16,256]{2,1,0:T(8,128)S(1)} %add.3), channel_id=1, replica_groups={{0,16,32,48,64,80,96,112,128,144,160,176,192,208,224,240},{8,24,40,56,7..., dimensions={0} | all-to-all | bytes 524288 | tf_op jit(solution)/shard_map/all_to_all | solution.py:256
  38.8 0.0 collective-permute-done.1.other
  38.8 0.6 first_share.1
  39.4 22.7 %all_to_all.26.shares = f32[8,16,1024]{2,1,0:T(8,128)S(1)} all-to-all(f32[8,16,1024]{2,1,0:T(8,128)S(1)} %get-tuple-element.17), channel_id=1, replica_groups=mesh['row'=32,'col'=8] {'col'}, dimensions={0} | all-to-all | bytes 1048576 | tf_op jit(solution)/shard_map/all_to_all | solution.py:256
  62.1 0.4 coupling.3
  62.5 11.4 %all_to_all.27.mine = f32[16,24,128]{2,1,0:T(8,128)S(1)} all-to-all(f32[16,24,128]{2,1,0:T(8,128)S(1)} %coupling.3), channel_id=1, replica_groups={{0,16,32,48,64,80,96,112,128,144,160,176,192,208,224,240},{8,24,40,56,7..., dimensions={0} | all-to-all | bytes 393216 | tf_op jit(solution)/shard_map/all_to_all | solution.py:256
  73.8 4.4 %collective-permute-start.2 = (f32[16,24,128]{2,1,0:T(8,128)S(1)}, f32[16,24,128]{2,1,0:T(8,128)S(1)}, u32[]{:S(2)}, u32[]{:S(2)}) collective-permute-start(f32[16,24,128]{2,1,0:T(8,128)S(1)} %all_to_all.27.mine), channel_id=1, source_target_pairs={{0,8},{8,0},{16,24},{24,16},{32,40},{40,32},{48,56},{56,48},{64,72... | collective-permute-start | bytes 589832 | tf_op jit(solution)/shard_map/ppermute | solution.py:294
  78.3 1.1 %collective-permute-done.2.theirs = f32[16,24,128]{2,1,0:T(8,128)S(1)} collective-permute-done((f32[16,24,128]{2,1,0:T(8,128)S(1)}, f32[16,24,128]{2,1,0:T(8,128)S(1)}, u32[]{:S(2)}, u32[]{:S(2)}) %collective-permute-start.2) | collective-permute-done | bytes 196640 | tf_op jit(solution)/shard_map/ppermute | solution.py:294
  79.3 0.0 copy-done
  79.3 0.3 second_share.1
  79.6 20.4 %all_to_all.28.shares = f32[8,64,256]{2,1,0:T(8,128)S(1)} all-to-all(f32[8,64,256]{2,1,0:T(8,128)S(1)} %get-tuple-element.20), channel_id=1, replica_groups=mesh['row'=32,'col'=8] {'col'}, dimensions={0} | all-to-all | bytes 1048576 | tf_op jit(solution)/shard_map/all_to_all | solution.py:256
  100.0 0.7 join.1
  (1 shorter events, 0.0 us)
Async XLA Ops:
  0.0 9.6 %copy-start.2 = (s32[2048]{0:T(1024)S(1)}, s32[2048]{0:T(1024)}, u32[]{:S(2)}) copy-start(s32[2048]{0:T(1024)} %param.7) | copy-start | bytes 24580
  0.0 9.6 %copy-start.1 = (f32[2,64,240]{2,1,0:T(8,128)S(1)}, f32[2,64,240]{2,1,0:T(8,128)}, u32[]{:S(2)}) copy-start(f32[2,64,240]{2,1,0:T(8,128)} %gradient_rhs.1) | copy-start | bytes 368644
  2.0 23.1 %all-to-all-start = ((f32[16,4,32,128]{3,2,1,0:T(8,128)}), f32[16,4,32,128]{3,2,1,0:T(8,128)S(1)}, u32[]{:S(2)}, u32[]{:S(2)}) async-start(f32[16,4,32,128]{3,2,1,0:T(8,128)} %prepare.1), calls=%async_computation | async-start | bytes 2097152 | tf_op jit(solution)/shard_map/all_to_all | solution.py:256
  9.6 69.7 %copy-start = (f32[2,2,32,128]{3,2,1,0:T(8,128)S(1)}, f32[2,2,32,128]{3,2,1,0:T(8,128)}, u32[]{:S(2)}) copy-start(f32[2,2,32,128]{3,2,1,0:T(8,128)} %inverse.3) | copy-start | bytes 196612
  18.3 2.2 %collective-permute-start = (f32[16,16,256]{2,1,0:T(8,128)S(1)}, f32[16,16,256]{2,1,0:T(8,128)S(1)}, u32[]{:S(2)}, u32[]{:S(2)}) collective-permute-start(f32[16,16,256]{2,1,0:T(8,128)S(1)} %get-tuple-element.14), channel_id=1, source_target_pairs={{0,8},{8,0},{16,24},{24,16},{32,40},{40,32},{48,56},{56,48},{64,72... | collective-permute-start | bytes 786440 | tf_op jit(solution)/shard_map/ppermute | solution.py:282
  25.1 13.8 %collective-permute-start.1 = (f32[16,4,32,128]{3,2,1,0:T(8,128)S(1)}, f32[16,4,32,128]{3,2,1,0:T(8,128)S(1)}, u32[]{:S(2)}, u32[]{:S(2)}) collective-permute-start(f32[16,4,32,128]{3,2,1,0:T(8,128)S(1)} %all-to-all-done.own), channel_id=1, source_target_pairs={{0,8},{8,0},{16,24},{24,16},{32,40},{40,32},{48,56},{56,48},{64,72... | collective-permute-start | bytes 3145736 | tf_op jit(solution)/shard_map/ppermute | solution.py:284
  73.8 5.5 %collective-permute-start.2 = (f32[16,24,128]{2,1,0:T(8,128)S(1)}, f32[16,24,128]{2,1,0:T(8,128)S(1)}, u32[]{:S(2)}, u32[]{:S(2)}) collective-permute-start(f32[16,24,128]{2,1,0:T(8,128)S(1)} %all_to_all.27.mine), channel_id=1, source_target_pairs={{0,8},{8,0},{16,24},{24,16},{32,40},{40,32},{48,56},{56,48},{64,72... | collective-permute-start | bytes 589832 | tf_op jit(solution)/shard_map/ppermute | solution.py:294

commit v4 on v3

--- a/solution.py
+++ b/solution.py
@@ -13,6 +13,10 @@
 CW = NB // COLS
 RW = NB // ROWS
 RC = 8
+LANES = 128
+TAIL = RHS - LANES
+FREE = LANES - TAIL
+GROUPS = 2 * RW // 8
 GRAD_ROWS = 2 * NB // ROWS
 DEPTH = 512
 AHEAD = 3
@@ -225,15 +229,31 @@
         place = slice(half * CHIPS * RC, (half + 1) * CHIPS * RC)
         first[:, place] = jnp.where(core == half, rows[0], rows[1])
         share = jnp.where(core == half, shares[0], shares[1])
-        for z in range(COLS):
-            copies[z, :, place] = share
+        if half == 0:
+            tiles = [share]
+        else:
+            tiles += [
+                jnp.concatenate(
+                    [share[g * 8 : (g + 1) * 8, :TAIL], share[-8:, g * FREE : (g + 1) * FREE]],
+                    axis=1,
+                )
+                for g in range(GROUPS - 1)
+            ]
+    packed = jnp.concatenate(tiles, axis=0)
+    for z in range(COLS):
+        copies[z] = packed
 
 
 def join_kernel(first, shares, out):
     second = jnp.sum(shares[...], axis=0)
+    tails = [second[2 * RW + g * 8 : 2 * RW + (g + 1) * 8] for g in range(GROUPS - 1)]
+    last = jnp.concatenate([tail[:, TAIL:] for tail in tails], axis=1)
+    tail = jnp.concatenate([tail[:, :TAIL] for tail in tails] + [last], axis=0)
     for c in range(2):
-        out[c, 0] = first[c * RW : (c + 1) * RW, :RHS]
-        out[c, 1] = second[c * RW : (c + 1) * RW, :RHS]
+        rows = slice(c * RW, (c + 1) * RW)
+        out[c, 0] = first[rows, :RHS]
+        out[c, 1, :, :LANES] = second[rows]
+        out[c, 1, :, LANES:] = tail[rows]
 
 
 def local(kernel, ins, shapes, name, scratch=(), limit=24):
@@ -293,7 +313,7 @@
     mine = exchange(packed, "row", SAME_CORE)
     theirs = lax.ppermute(mine, "row", OTHER_CORE)
     first, copies = local(
-        second_kernel, [VMEM] * 3, [(2 * RW, ROWS * RC), (COLS, 2 * RW, ROWS * RC)], "second_share"
+        second_kernel, [VMEM] * 3, [(2 * RW, ROWS * RC), (COLS, 2 * RW + 8 * (GROUPS - 1), LANES)], "second_share"
     )(mine, theirs, block_inverse)
     shares = exchange(copies, "col")
     (solved,) = local(join_kernel, [VMEM] * 2, [(2, 2, RW, RHS)], "join")(first, shares)

time: 101 us -> 100 us (0.990)
  no operation moved by 1% of the time
where the time goes in v4:
time: 100 us
  blocking collectives  64.3 us (64%)
  starting transfers between devices  16.2 us (16%)
  Pallas kernels  12.7 us (13%)
  waiting for transfers between devices  6.78 us (7%)
    all_to_all x4, blocking collectives, exchange(): return lax.all_to_all(x, axis, 0, 0, axis_index_groups=groups, tiled=True)  64.3 us
    pallas_call x1, Pallas kernels, column_terms(): pl.pallas_call(sums_kernel, out_shape=[jax.ShapeDtypeStruct((CHIPS, 2 * R...  8.69 us
    all_to_all x1, starting transfers between devices, exchange(): return lax.all_to_all(x, axis, 0, 0, axis_index_groups=groups, tiled=True)  7.6 us
    all_to_all x1, waiting for transfers between devices, exchange(): return lax.all_to_all(x, axis, 0, 0, axis_index_groups=groups, tiled=True)  4.55 us
    ppermute x1, starting transfers between devices, on_device(): theirs = lax.ppermute(mine, 'row', OTHER_CORE)  4.42 us
    ppermute x1, starting transfers between devices, on_device(): other = lax.ppermute(own, 'row', OTHER_CORE)  3.14 us
  transfers between devices with their start and end apart: 4, of which 3 were waited for; matrix products, arithmetic and copies ran while one was open for 0% of the time, Pallas kernels for 9%

profile of v4, /device:TPU:1, one launch (start us, length us, event | category | flops | bytes accessed | tf_op | source)
XLA Modules:
  0.0 100.1 jit_solution(657439121711632537)
XLA Ops:
  0.0 0.0 copy-start.2
  0.0 0.0 copy-start.1
  0.0 1.9 %prepare.1 = f32[16,4,32,128]{3,2,1,0:T(8,128)} custom-call(f32[2,2,32,128]{3,2,1,0:T(8,128)} %inverse.3, f32[2,32,128]{2,1,0:T(8,128)} %coupling.2), custom_call_target="tpu_custom_call" | custom-call | flops 10000000000 | bytes 33554432 | tf_op jit(solution)/shard_map/prepare/pallas_call | solution.py:280
  2.0 7.6 %all-to-all-start = ((f32[16,4,32,128]{3,2,1,0:T(8,128)}), f32[16,4,32,128]{3,2,1,0:T(8,128)S(1)}, u32[]{:S(2)}, u32[]{:S(2)}) async-start(f32[16,4,32,128]{3,2,1,0:T(8,128)} %prepare.1), calls=%async_computation | async-start | bytes 2097152 | tf_op jit(solution)/shard_map/all_to_all | solution.py:276
  9.6 0.0 copy-done.2
  9.6 0.0 copy-done.1
  9.6 0.0 copy-start
  9.6 8.7 %column_terms.1 = (f32[16,16,256]{2,1,0:T(8,128)S(1)}, f32[16,16,256]{2,1,0:T(8,128)S(1)}) custom-call(f32[2,240,4096]{2,1,0:T(8,128)} %bitcast.5, f32[2,8192,128]{2,1,0:T(8,128)} %bitcast.4, f32[2,64,240]{2,1,0:T(8,128)S(1)} %copy-done.1, s32[16,128]{1,0:T(8,128)S(1)} %bitcast.3), custom_call_target="tpu_custom_call" | custom-call | flops 6039797760 | bytes 16252928 | tf_op jit(solution)/shard_map/column_terms/pallas_call | solution.py:149
  18.3 1.0 %collective-permute-start = (f32[16,16,256]{2,1,0:T(8,128)S(1)}, f32[16,16,256]{2,1,0:T(8,128)S(1)}, u32[]{:S(2)}, u32[]{:S(2)}) collective-permute-start(f32[16,16,256]{2,1,0:T(8,128)S(1)} %get-tuple-element.14), channel_id=1, source_target_pairs={{0,8},{8,0},{16,24},{24,16},{32,40},{40,32},{48,56},{56,48},{64,72... | collective-permute-start | bytes 786440 | tf_op jit(solution)/shard_map/ppermute | solution.py:302
  19.3 1.2 %collective-permute-done = f32[16,16,256]{2,1,0:T(8,128)S(1)} collective-permute-done((f32[16,16,256]{2,1,0:T(8,128)S(1)}, f32[16,16,256]{2,1,0:T(8,128)S(1)}, u32[]{:S(2)}, u32[]{:S(2)}) %collective-permute-start) | collective-permute-done | bytes 262176 | tf_op jit(solution)/shard_map/ppermute | solution.py:302
  20.5 4.5 %all-to-all-done.own = f32[16,4,32,128]{3,2,1,0:T(8,128)S(1)} async-done(((f32[16,4,32,128]{3,2,1,0:T(8,128)}), f32[16,4,32,128]{3,2,1,0:T(8,128)S(1)}, u32[]{:S(2)}, u32[]{:S(2)}) %all-to-all-start) | async-done | bytes 1048608 | tf_op jit(solution)/shard_map/all_to_all | solution.py:276
  25.1 3.1 %collective-permute-start.1 = (f32[16,4,32,128]{3,2,1,0:T(8,128)S(1)}, f32[16,4,32,128]{3,2,1,0:T(8,128)S(1)}, u32[]{:S(2)}, u32[]{:S(2)}) collective-permute-start(f32[16,4,32,128]{3,2,1,0:T(8,128)S(1)} %all-to-all-done.own), channel_id=1, source_target_pairs={{0,8},{8,0},{16,24},{24,16},{32,40},{40,32},{48,56},{56,48},{64,72... | collective-permute-start | bytes 3145736 | tf_op jit(solution)/shard_map/ppermute | solution.py:304
  28.2 10.6 %all_to_all.25.terms = f32[16,16,256]{2,1,0:T(8,128)S(1)} all-to-all(f32[16,16,256]{2,1,0:T(8,128)S(1)} %add.3), channel_id=1, replica_groups={{0,16,32,48,64,80,96,112,128,144,160,176,192,208,224,240},{8,24,40,56,7..., dimensions={0} | all-to-all | bytes 524288 | tf_op jit(solution)/shard_map/all_to_all | solution.py:276
  38.8 0.0 collective-permute-done.1.other
  38.8 0.6 first_share.1
  39.4 22.7 %all_to_all.26.shares = f32[8,16,1024]{2,1,0:T(8,128)S(1)} all-to-all(f32[8,16,1024]{2,1,0:T(8,128)S(1)} %get-tuple-element.17), channel_id=1, replica_groups=mesh['row'=32,'col'=8] {'col'}, dimensions={0} | all-to-all | bytes 1048576 | tf_op jit(solution)/shard_map/all_to_all | solution.py:276
  62.1 0.4 coupling.3
  62.5 11.4 %all_to_all.27.mine = f32[16,24,128]{2,1,0:T(8,128)S(1)} all-to-all(f32[16,24,128]{2,1,0:T(8,128)S(1)} %coupling.3), channel_id=1, replica_groups={{0,16,32,48,64,80,96,112,128,144,160,176,192,208,224,240},{8,24,40,56,7..., dimensions={0} | all-to-all | bytes 393216 | tf_op jit(solution)/shard_map/all_to_all | solution.py:276
  73.8 4.4 %collective-permute-start.2 = (f32[16,24,128]{2,1,0:T(8,128)S(1)}, f32[16,24,128]{2,1,0:T(8,128)S(1)}, u32[]{:S(2)}, u32[]{:S(2)}) collective-permute-start(f32[16,24,128]{2,1,0:T(8,128)S(1)} %all_to_all.27.mine), channel_id=1, source_target_pairs={{0,8},{8,0},{16,24},{24,16},{32,40},{40,32},{48,56},{56,48},{64,72... | collective-permute-start | bytes 589832 | tf_op jit(solution)/shard_map/ppermute | solution.py:314
  78.3 1.1 %collective-permute-done.2.theirs = f32[16,24,128]{2,1,0:T(8,128)S(1)} collective-permute-done((f32[16,24,128]{2,1,0:T(8,128)S(1)}, f32[16,24,128]{2,1,0:T(8,128)S(1)}, u32[]{:S(2)}, u32[]{:S(2)}) %collective-permute-start.2) | collective-permute-done | bytes 196640 | tf_op jit(solution)/shard_map/ppermute | solution.py:314
  79.3 0.0 copy-done
  79.3 0.3 second_share.1
  79.7 19.7 %all_to_all.28.shares = f32[8,120,128]{2,1,0:T(8,128)S(1)} all-to-all(f32[8,120,128]{2,1,0:T(8,128)S(1)} %get-tuple-element.20), channel_id=1, replica_groups=mesh['row'=32,'col'=8] {'col'}, dimensions={0} | all-to-all | bytes 983040 | tf_op jit(solution)/shard_map/all_to_all | solution.py:276
  99.3 0.7 join.1
  (1 shorter events, 0.0 us)
Async XLA Ops:
  0.0 9.6 %copy-start.2 = (s32[2048]{0:T(1024)S(1)}, s32[2048]{0:T(1024)}, u32[]{:S(2)}) copy-start(s32[2048]{0:T(1024)} %param.7) | copy-start | bytes 24580
  0.0 9.6 %copy-start.1 = (f32[2,64,240]{2,1,0:T(8,128)S(1)}, f32[2,64,240]{2,1,0:T(8,128)}, u32[]{:S(2)}) copy-start(f32[2,64,240]{2,1,0:T(8,128)} %gradient_rhs.1) | copy-start | bytes 368644
  2.0 23.1 %all-to-all-start = ((f32[16,4,32,128]{3,2,1,0:T(8,128)}), f32[16,4,32,128]{3,2,1,0:T(8,128)S(1)}, u32[]{:S(2)}, u32[]{:S(2)}) async-start(f32[16,4,32,128]{3,2,1,0:T(8,128)} %prepare.1), calls=%async_computation | async-start | bytes 2097152 | tf_op jit(solution)/shard_map/all_to_all | solution.py:276
  9.6 69.7 %copy-start = (f32[2,2,32,128]{3,2,1,0:T(8,128)S(1)}, f32[2,2,32,128]{3,2,1,0:T(8,128)}, u32[]{:S(2)}) copy-start(f32[2,2,32,128]{3,2,1,0:T(8,128)} %inverse.3) | copy-start | bytes 196612
  18.3 2.2 %collective-permute-start = (f32[16,16,256]{2,1,0:T(8,128)S(1)}, f32[16,16,256]{2,1,0:T(8,128)S(1)}, u32[]{:S(2)}, u32[]{:S(2)}) collective-permute-start(f32[16,16,256]{2,1,0:T(8,128)S(1)} %get-tuple-element.14), channel_id=1, source_target_pairs={{0,8},{8,0},{16,24},{24,16},{32,40},{40,32},{48,56},{56,48},{64,72... | collective-permute-start | bytes 786440 | tf_op jit(solution)/shard_map/ppermute | solution.py:302
  25.1 13.8 %collective-permute-start.1 = (f32[16,4,32,128]{3,2,1,0:T(8,128)S(1)}, f32[16,4,32,128]{3,2,1,0:T(8,128)S(1)}, u32[]{:S(2)}, u32[]{:S(2)}) collective-permute-start(f32[16,4,32,128]{3,2,1,0:T(8,128)S(1)} %all-to-all-done.own), channel_id=1, source_target_pairs={{0,8},{8,0},{16,24},{24,16},{32,40},{40,32},{48,56},{56,48},{64,72... | collective-permute-start | bytes 3145736 | tf_op jit(solution)/shard_map/ppermute | solution.py:304
  73.8 5.5 %collective-permute-start.2 = (f32[16,24,128]{2,1,0:T(8,128)S(1)}, f32[16,24,128]{2,1,0:T(8,128)S(1)}, u32[]{:S(2)}, u32[]{:S(2)}) collective-permute-start(f32[16,24,128]{2,1,0:T(8,128)S(1)} %all_to_all.27.mine), channel_id=1, source_target_pairs={{0,8},{8,0},{16,24},{24,16},{32,40},{40,32},{48,56},{56,48},{64,72... | collective-permute-start | bytes 589832 | tf_op jit(solution)/shard_map/ppermute | solution.py:314
